TPU v7x, 128 devices: a whole 4x4x4 slice. The times are simulated.
128 devices in a mesh: chan: 4 (over x), tile: 32 (over y, z, core).
Axes of the slice: x: 4, y: 4, z: 4, core: 2. Of those that a mesh axis runs over, the one named last changes fastest.
Arguments:
- voltages: bfloat16 [2, 128, 2048, 512], P(None, None, ('chan', 'tile')), may hold values from -6 to 6
- tile_pairs: int32 [528, 2], replicated, may hold values from 0 to 31, as said below
Outputs:
- visibilities: float32 [528, 128, 64, 128], P(None, ('chan', 'tile'))
Inputs may be any that keep to these rules, and one draw needn't show every extreme that they name: `tile_pairs`: every pair of panels (p, q) with p <= q occurs in exactly one row; in every row the first entry is at most the second.
All inputs are finite; a program needn't handle non-finite values.
Results may differ from a plain program's by a relative error of at most 0.0003.
Values may be sent and summed in bfloat16 or wider, within the bound.
No kernel may reach another device: no remote copies, remote signals or barrier semaphores. Data moves between devices by JAX's collectives and lax.ppermute only.
A program may use at most 320 MiB of HBM per device.

v0:
```python
import jax
import jax.numpy as jnp
from jax import lax
from jax.sharding import PartitionSpec as P

PANELS = 32
TBLOCK = 128
PANEL = 64


def accumulate(running, turned):
    real_part = turned[0]
    imag_part = turned[1]
    left_all = jnp.concatenate((real_part, imag_part), axis=-1)
    rotated = jnp.concatenate((-imag_part, real_part), axis=-1)
    right_all = jnp.concatenate((left_all, rotated), axis=1)
    product = lax.dot_general(
        left_all, right_all, (((2,), (2,)), ((0,), (0,))), preferred_element_type=jnp.float32
    )
    return running + product


def body(voltages, tile_pairs):
    chans_here = voltages.shape[1] // (lax.axis_size("chan") * lax.axis_size("tile"))
    local_inputs = voltages.shape[2]
    spectra_all = voltages.shape[3]
    turn_count = spectra_all // TBLOCK
    inputs_all = PANELS * PANEL
    first_panel = tile_pairs[:, 0]
    second_panel = tile_pairs[:, 1]
    running = jnp.zeros((chans_here, inputs_all, 2 * inputs_all), jnp.float32)

    def advance(index, current):
        piece = lax.dynamic_slice_in_dim(voltages, index * TBLOCK, TBLOCK, 3)
        shaped = piece.reshape(2, voltages.shape[1], 1, local_inputs, TBLOCK)
        turned = lax.all_to_all(shaped, ("chan", "tile"), split_axis=1, concat_axis=2, tiled=True)
        turned = turned.reshape(2, chans_here, inputs_all, TBLOCK)
        return accumulate(current, turned)

    running = lax.fori_loop(0, turn_count, advance, running)
    grid = running.reshape(chans_here, PANELS, PANEL, 2, PANELS, PANEL)
    picked = grid[:, first_panel, :, :, second_panel, :]
    picked = picked.reshape(tile_pairs.shape[0], chans_here, PANEL, 2 * PANEL)
    return picked * spectra_all ** (-0.5)


def solution(mesh):
    placed = (P(None, None, ("chan", "tile"), None), P())
    return jax.shard_map(
        body,
        mesh=mesh,
        in_specs=placed,
        out_specs=P(None, ("chan", "tile"), None, None),
        check_vma=False,
    )
```

profile of v0, /device:TPU:1, one launch (start us, length us, event | category | flops | bytes accessed | tf_op | source)
XLA Modules:
  0.0 428.4 jit_solution(4955212542927331651)
XLA Ops:
  0.0 199.4 %while.14 = (s32[]{:T(128)}, f32[1,2048,4096]{2,1,0:T(8,128)}, bf16[2,128,16,512]{3,2,1,0:T(8,128)(2,1)}, s32[]{:T(128)}, s32[]{:T(128)}, /*index=5*/s32[]{:T(128)}, s32[]{:T(128)}) while((s32[]{:T(128)}, f32[1,2048,4096]{2,1,0:T(8,128)}, bf16[2,128,16,512]{3,2,1,0:T(8,128)(2,1)}, s32[]{:T(128)}, s32[]{:T(128)}, ...), condition=%wide.region_1.0_spmd.clone, body=%wide.region_0.0_spmd.clone.sunk | while | flops 4322492416 | bytes 77070504 | solution.py:40
  0.0 2.4 copy_bitcast_fusion.2
  2.4 11.5 %all-to-all-start = ((bf16[2,128,1,16,128]{4,3,0,2,1:T(8,128)(2,1)}), bf16[2,128,1,16,128]{4,3,0,2,1:T(8,128)(2,1)S(1)}, u32[]{:S(2)}, u32[]{:S(2)}) async-start(bf16[2,128,1,16,128]{4,3,0,2,1:T(8,128)(2,1)} %copy_bitcast_fusion.2), calls=%async_computation | async-start | bytes 2097152 | tf_op jit(solution)/shard_map/while/body/eval_jaxpr/all_to_all | solution.py:36
  13.9 19.3 %all-to-all-done = bf16[2,128,1,16,128]{4,3,0,2,1:T(8,128)(2,1)S(1)} async-done(((bf16[2,128,1,16,128]{4,3,0,2,1:T(8,128)(2,1)}), bf16[2,128,1,16,128]{4,3,0,2,1:T(8,128)(2,1)S(1)}, u32[]{:S(2)}, u32[]{:S(2)}) %all-to-all-start) | async-done | bytes 1048608 | tf_op jit(solution)/shard_map/while/body/eval_jaxpr/all_to_all | solution.py:36
  33.2 0.2 fusion.17
  33.3 0.1 neg.17
  33.5 13.1 %bitcast_add_fusion.2 = f32[1,2048,4096]{2,1,0:T(8,128)} fusion(f32[1,2048,4096]{2,1,0:T(8,128)} %get-tuple-element.127, pred[]{:T(512)S(6)} %compare.3, bf16[1,2048,128]{2,1,0:T(8,128)(2,1)S(1)} %bitcast.27, bf16[1,2048,128]{2,1,0:T(8,128)(2,1)S(1)} %neg.17, bf16[1,2048,128]{2,1,0:T(8,128)(2,1)S(1)} %bitcast.26), kind=kOutput, calls=%fused_computation.1.clone.1 | convolution fusion | flops 4322230272 | bytes 68681728 | tf_op jit(solution)/shard_map/while/body/eval_jaxpr/dot_general | solution.py:17
  46.6 2.4 copy_bitcast_fusion.2
  49.0 4.6 %all-to-all-start = ((bf16[2,128,1,16,128]{4,3,0,2,1:T(8,128)(2,1)}), bf16[2,128,1,16,128]{4,3,0,2,1:T(8,128)(2,1)S(1)}, u32[]{:S(2)}, u32[]{:S(2)}) async-start(bf16[2,128,1,16,128]{4,3,0,2,1:T(8,128)(2,1)} %copy_bitcast_fusion.2), calls=%async_computation | async-start | bytes 2097152 | tf_op jit(solution)/shard_map/while/body/eval_jaxpr/all_to_all | solution.py:36
  53.6 19.4 %all-to-all-done = bf16[2,128,1,16,128]{4,3,0,2,1:T(8,128)(2,1)S(1)} async-done(((bf16[2,128,1,16,128]{4,3,0,2,1:T(8,128)(2,1)}), bf16[2,128,1,16,128]{4,3,0,2,1:T(8,128)(2,1)S(1)}, u32[]{:S(2)}, u32[]{:S(2)}) %all-to-all-start) | async-done | bytes 1048608 | tf_op jit(solution)/shard_map/while/body/eval_jaxpr/all_to_all | solution.py:36
  73.0 0.2 fusion.17
  73.2 0.1 neg.17
  73.3 24.3 %bitcast_add_fusion.2 = f32[1,2048,4096]{2,1,0:T(8,128)} fusion(f32[1,2048,4096]{2,1,0:T(8,128)} %get-tuple-element.127, pred[]{:T(512)S(6)} %compare.3, bf16[1,2048,128]{2,1,0:T(8,128)(2,1)S(1)} %bitcast.27, bf16[1,2048,128]{2,1,0:T(8,128)(2,1)S(1)} %neg.17, bf16[1,2048,128]{2,1,0:T(8,128)(2,1)S(1)} %bitcast.26), kind=kOutput, calls=%fused_computation.1.clone.1 | convolution fusion | flops 4322230272 | bytes 68681728 | tf_op jit(solution)/shard_map/while/body/eval_jaxpr/dot_general | solution.py:17
  97.5 2.4 copy_bitcast_fusion.2
  99.9 4.6 %all-to-all-start = ((bf16[2,128,1,16,128]{4,3,0,2,1:T(8,128)(2,1)}), bf16[2,128,1,16,128]{4,3,0,2,1:T(8,128)(2,1)S(1)}, u32[]{:S(2)}, u32[]{:S(2)}) async-start(bf16[2,128,1,16,128]{4,3,0,2,1:T(8,128)(2,1)} %copy_bitcast_fusion.2), calls=%async_computation | async-start | bytes 2097152 | tf_op jit(solution)/shard_map/while/body/eval_jaxpr/all_to_all | solution.py:36
  104.5 19.4 %all-to-all-done = bf16[2,128,1,16,128]{4,3,0,2,1:T(8,128)(2,1)S(1)} async-done(((bf16[2,128,1,16,128]{4,3,0,2,1:T(8,128)(2,1)}), bf16[2,128,1,16,128]{4,3,0,2,1:T(8,128)(2,1)S(1)}, u32[]{:S(2)}, u32[]{:S(2)}) %all-to-all-start) | async-done | bytes 1048608 | tf_op jit(solution)/shard_map/while/body/eval_jaxpr/all_to_all | solution.py:36
  123.9 0.2 fusion.17
  124.1 0.1 neg.17
  124.2 24.3 %bitcast_add_fusion.2 = f32[1,2048,4096]{2,1,0:T(8,128)} fusion(f32[1,2048,4096]{2,1,0:T(8,128)} %get-tuple-element.127, pred[]{:T(512)S(6)} %compare.3, bf16[1,2048,128]{2,1,0:T(8,128)(2,1)S(1)} %bitcast.27, bf16[1,2048,128]{2,1,0:T(8,128)(2,1)S(1)} %neg.17, bf16[1,2048,128]{2,1,0:T(8,128)(2,1)S(1)} %bitcast.26), kind=kOutput, calls=%fused_computation.1.clone.1 | convolution fusion | flops 4322230272 | bytes 68681728 | tf_op jit(solution)/shard_map/while/body/eval_jaxpr/dot_general | solution.py:17
  148.5 2.4 copy_bitcast_fusion.2
  150.8 4.6 %all-to-all-start = ((bf16[2,128,1,16,128]{4,3,0,2,1:T(8,128)(2,1)}), bf16[2,128,1,16,128]{4,3,0,2,1:T(8,128)(2,1)S(1)}, u32[]{:S(2)}, u32[]{:S(2)}) async-start(bf16[2,128,1,16,128]{4,3,0,2,1:T(8,128)(2,1)} %copy_bitcast_fusion.2), calls=%async_computation | async-start | bytes 2097152 | tf_op jit(solution)/shard_map/while/body/eval_jaxpr/all_to_all | solution.py:36
  155.4 19.4 %all-to-all-done = bf16[2,128,1,16,128]{4,3,0,2,1:T(8,128)(2,1)S(1)} async-done(((bf16[2,128,1,16,128]{4,3,0,2,1:T(8,128)(2,1)}), bf16[2,128,1,16,128]{4,3,0,2,1:T(8,128)(2,1)S(1)}, u32[]{:S(2)}, u32[]{:S(2)}) %all-to-all-start) | async-done | bytes 1048608 | tf_op jit(solution)/shard_map/while/body/eval_jaxpr/all_to_all | solution.py:36
  174.9 0.2 fusion.17
  175.0 0.1 neg.17
  175.2 24.3 %bitcast_add_fusion.2 = f32[1,2048,4096]{2,1,0:T(8,128)} fusion(f32[1,2048,4096]{2,1,0:T(8,128)} %get-tuple-element.127, pred[]{:T(512)S(6)} %compare.3, bf16[1,2048,128]{2,1,0:T(8,128)(2,1)S(1)} %bitcast.27, bf16[1,2048,128]{2,1,0:T(8,128)(2,1)S(1)} %neg.17, bf16[1,2048,128]{2,1,0:T(8,128)(2,1)S(1)} %bitcast.26), kind=kOutput, calls=%fused_computation.1.clone.1 | convolution fusion | flops 4322230272 | bytes 68681728 | tf_op jit(solution)/shard_map/while/body/eval_jaxpr/dot_general | solution.py:17
  199.4 52.7 %reshape.66 = f32[32,64,2,32,64]{4,3,2,1,0:T(8,128)} reshape(f32[1,2048,4096]{2,1,0:T(8,128)} %get-tuple-element.69) | data formatting | bytes 67108864 | tf_op jit(solution)/shard_map/reshape | solution.py:41
  252.1 0.0 copy-start
  252.1 56.3 %copy.13 = f32[32,64,2,32,64]{4,1,3,2,0:T(8,128)} copy(f32[32,64,2,32,64]{4,3,2,1,0:T(8,128)} %reshape.66) | data formatting | bytes 67108864 | tf_op jit(solution)/shard_map/reshape | solution.py:41
  308.4 0.0 copy-done
  308.4 50.5 %gather_fusion = f32[528,64,2,64]{3,1,2,0:T(8,128)} fusion(f32[32,64,2,32,64]{4,1,3,2,0:T(8,128)} %copy.13, s32[528]{0:T(1024)S(1)} %fusion.14), kind=kCustom, calls=%fused_computation | custom fusion | bytes 34607232 | tf_op jit(solution)/shard_map/gather | solution.py:42
  358.9 32.3 %copy.14 = f32[528,64,2,64]{0,3,2,1:T(8,128)} copy(f32[528,64,2,64]{3,1,2,0:T(8,128)} %gather_fusion) | data formatting | bytes 34603008 | tf_op jit(solution)/shard_map/gather | solution.py:42
  391.2 17.3 %broadcast_multiply_fusion = f32[528,64,2,64]{0,3,2,1:T(8,128)} fusion(f32[528,64,2,64]{0,3,2,1:T(8,128)} %copy.14), kind=kLoop, calls=%fused_computation.15 | loop fusion | flops 4325376 | bytes 34603008 | tf_op jit(solution)/shard_map/mul | solution.py:44
  408.5 19.9 %copy.15 = f32[528,1,64,128]{3,2,1,0:T(8,128)} copy(f32[528,1,64,128]{0,3,2,1:T(8,128)} %bitcast.28) | data formatting | bytes 34603008 | tf_op jit(solution)/shard_map/mul | solution.py:44
  (2 shorter events, 0.0 us)
Async XLA Ops:
  2.4 30.8 %all-to-all-start = ((bf16[2,128,1,16,128]{4,3,0,2,1:T(8,128)(2,1)}), bf16[2,128,1,16,128]{4,3,0,2,1:T(8,128)(2,1)S(1)}, u32[]{:S(2)}, u32[]{:S(2)}) async-start(bf16[2,128,1,16,128]{4,3,0,2,1:T(8,128)(2,1)} %copy_bitcast_fusion.2), calls=%async_computation | async-start | bytes 2097152 | tf_op jit(solution)/shard_map/while/body/eval_jaxpr/all_to_all | solution.py:36
  49.0 24.0 %all-to-all-start = ((bf16[2,128,1,16,128]{4,3,0,2,1:T(8,128)(2,1)}), bf16[2,128,1,16,128]{4,3,0,2,1:T(8,128)(2,1)S(1)}, u32[]{:S(2)}, u32[]{:S(2)}) async-start(bf16[2,128,1,16,128]{4,3,0,2,1:T(8,128)(2,1)} %copy_bitcast_fusion.2), calls=%async_computation | async-start | bytes 2097152 | tf_op jit(solution)/shard_map/while/body/eval_jaxpr/all_to_all | solution.py:36
  99.9 24.0 %all-to-all-start = ((bf16[2,128,1,16,128]{4,3,0,2,1:T(8,128)(2,1)}), bf16[2,128,1,16,128]{4,3,0,2,1:T(8,128)(2,1)S(1)}, u32[]{:S(2)}, u32[]{:S(2)}) async-start(bf16[2,128,1,16,128]{4,3,0,2,1:T(8,128)(2,1)} %copy_bitcast_fusion.2), calls=%async_computation | async-start | bytes 2097152 | tf_op jit(solution)/shard_map/while/body/eval_jaxpr/all_to_all | solution.py:36
  150.8 24.0 %all-to-all-start = ((bf16[2,128,1,16,128]{4,3,0,2,1:T(8,128)(2,1)}), bf16[2,128,1,16,128]{4,3,0,2,1:T(8,128)(2,1)S(1)}, u32[]{:S(2)}, u32[]{:S(2)}) async-start(bf16[2,128,1,16,128]{4,3,0,2,1:T(8,128)(2,1)} %copy_bitcast_fusion.2), calls=%async_computation | async-start | bytes 2097152 | tf_op jit(solution)/shard_map/while/body/eval_jaxpr/all_to_all | solution.py:36
  252.1 56.3 %copy-start = (s32[528,2]{0,1:T(2,128)S(1)}, s32[528,2]{0,1:T(2,128)}, u32[]{:S(2)}) copy-start(s32[528,2]{0,1:T(2,128)} %param.5) | copy-start | bytes 12676
where the time goes:
time: 431 us; the launch traced here: 428 us
  local copies, waits for them, and re-layouts  222 us (52%)
  matrix products  85.9 us (20%)
  waiting for transfers between devices  77.5 us (18%)
  starting transfers between devices  25.3 us (6%)
  other arithmetic  17.8 us (4%)
    reshape x2, local copies, waits for them, and re-layouts, body(): grid = running.reshape(chans_here, PANELS, PANEL, 2, PANELS, PANEL)  109 us
    dot_general x4, matrix products, accumulate(): lax.dot_general(left_all, right_all, (((2,), (2,)), ((0,), (0,))), prefer...  85.9 us
    gather x2, local copies, waits for them, and re-layouts, body(): picked = grid[:, first_panel, :, :, second_panel, :]  82.7 us
    all_to_all x4, waiting for transfers between devices, advance(): lax.all_to_all(shaped, ('chan', 'tile'), split_axis=1, concat_axis=2, til...  77.5 us
    all_to_all x4, starting transfers between devices, advance(): lax.all_to_all(shaped, ('chan', 'tile'), split_axis=1, concat_axis=2, til...  25.3 us
    mul x1, local copies, waits for them, and re-layouts, body(): return picked * spectra_all ** (-0.5)  19.9 us
    mul x1, other arithmetic, body(): return picked * spectra_all ** (-0.5)  17.3 us
    reshape x4, local copies, waits for them, and re-layouts, advance(): shaped = piece.reshape(2, voltages.shape[1], 1, local_inputs, TBLOCK)  9.49 us
  transfers between devices with their start and end apart: 4, of which 4 were waited for; matrix products, arithmetic and copies ran while one was open for 0% of the time, Pallas kernels for 0%

commit v1 on v0

v1 whole, which is shorter than its diff:
```python
import jax
import jax.numpy as jnp
from jax import lax
from jax.experimental import pallas as pl
from jax.experimental.pallas import tpu as pltpu
from jax.sharding import PartitionSpec as P

AXES = ("chan", "tile")
PANEL = 64
GROUP = 4


def visibilities(slot_ref, x_ref, out_ref, stacked, staged, sem, *, panels, scale):
    devices_per_panel = PANEL // x_ref.shape[2]
    spectra = x_ref.shape[3]
    blocks = panels // GROUP
    rows = GROUP * PANEL

    @pl.loop(0, panels)
    def _(p):
        here = pl.ds(p * devices_per_panel, devices_per_panel)
        real = x_ref[here, 0].reshape(PANEL, spectra)
        imag = x_ref[here, 1].reshape(PANEL, spectra)
        stacked[p, :PANEL, :spectra] = real
        stacked[p, :PANEL, spectra:] = imag
        stacked[p, PANEL:, :spectra] = -imag
        stacked[p, PANEL:, spectra:] = real

    def out_copy(place, i, j, a, b):
        slot = slot_ref[(i * GROUP + a) * panels + j * GROUP + b]
        return pltpu.make_async_copy(staged.at[place, a, b], out_ref.at[slot, 0], sem)

    @pl.loop(0, blocks)
    def _(j):
        right = stacked[pl.ds(j * GROUP, GROUP)].reshape(2 * rows, 2 * spectra)

        def pair(i):
            place = j * (j + 1) // 2 + i
            left = stacked[pl.ds(i * GROUP, GROUP), :PANEL].reshape(rows, 2 * spectra)
            product = lax.dot_general(
                left, right, (((1,), (1,)), ((), ())), preferred_element_type=jnp.float32
            )
            product = product * scale
            for a in range(GROUP):
                for b in range(GROUP):
                    staged[place, a, b] = product[
                        a * PANEL : (a + 1) * PANEL, b * 2 * PANEL : (b + 1) * 2 * PANEL
                    ]
            return place

        @pl.loop(0, j)
        def _(i):
            place = pair(i)
            for a in range(GROUP):
                for b in range(GROUP):
                    out_copy(place, i, j, a, b).start()

        place = pair(j)
        for a in range(GROUP):
            for b in range(a, GROUP):
                out_copy(place, j, j, a, b).start()

    pltpu.make_async_copy(out_ref, out_ref, sem).wait()


def body(voltages, tile_pairs):
    parts, chans, inputs_here, spectra = voltages.shape
    devices = lax.axis_size("chan") * lax.axis_size("tile")
    slots = tile_pairs.shape[0]
    panels = devices * inputs_here // PANEL
    blocks = panels // GROUP

    place = tile_pairs[:, 0] * panels + tile_pairs[:, 1]
    found = place[None, :] == jnp.arange(panels * panels, dtype=jnp.int32)[:, None]
    slot_of = jnp.sum(
        jnp.where(found, jnp.arange(slots, dtype=jnp.int32)[None, :], 0), axis=1
    )

    turned = lax.all_to_all(
        voltages.transpose(1, 0, 2, 3), AXES, split_axis=0, concat_axis=0, tiled=True
    )
    return pl.pallas_call(
        lambda *refs: visibilities(*refs, panels=panels, scale=spectra**-0.5),
        out_shape=jax.ShapeDtypeStruct((slots, 1, PANEL, 2 * PANEL), jnp.float32),
        in_specs=[
            pl.BlockSpec(memory_space=pltpu.SMEM),
            pl.BlockSpec(memory_space=pltpu.VMEM),
        ],
        out_specs=pl.BlockSpec(memory_space=pl.ANY),
        scratch_shapes=[
            pltpu.VMEM((panels, 2 * PANEL, 2 * spectra), jnp.bfloat16),
            pltpu.VMEM((blocks * (blocks + 1) // 2, GROUP, GROUP, PANEL, 2 * PANEL), jnp.float32),
            pltpu.SemaphoreType.DMA,
        ],
        compiler_params=pltpu.CompilerParams(vmem_limit_bytes=48 * 2**20),
        cost_estimate=pl.CostEstimate(
            flops=2 * slots * PANEL * 2 * PANEL * 2 * spectra,
            bytes_accessed=slots * PANEL * 2 * PANEL * 4,
            transcendentals=0,
        ),
        name="visibilities",
    )(slot_of, turned)


def solution(mesh):
    placed = (P(None, None, AXES, None), P())
    return jax.shard_map(
        body,
        mesh=mesh,
        in_specs=placed,
        out_specs=P(None, AXES, None, None),
        check_vma=False,
    )
```

time: 431 us -> 91.6 us (0.21)
  local copies, waits for them, and re-layouts: 222 us -> 4.85 us
  matrix products: 85.9 us -> 0 us
  waiting for transfers between devices: 77.5 us -> 52.4 us
  Pallas kernels: 0 us -> 21.8 us
  other arithmetic: 17.8 us -> 0.31 us
  starting transfers between devices: 25.3 us -> 12 us
    reshape x6 -> x0, local copies, waits for them, and re-layouts: 118 us -> none  [the longest x2 109 us: body(): grid = running.reshape(chans_here, PANELS, PANEL, 2, PANELS, PANEL)]
    dot_general x4 -> x0, matrix products: 85.9 us -> none  [accumulate(): lax.dot_general(left_all, right_all, (((2,), (2,)), ((0,), (0,))), prefer...]
    gather x2 -> x0, local copies, waits for them, and re-layouts: 82.7 us -> none  [body(): picked = grid[:, first_panel, :, :, second_panel, :]]
    all_to_all x4 -> x1, waiting for transfers between devices: 77.5 us -> 52.4 us  [body(): lax.all_to_all(voltages.transpose(1, 0, 2, 3), AXES, split_axis=0, concat...]
    pallas_call x0 -> x1, Pallas kernels: none -> 21.8 us  [body(): pl.pallas_call(lambda *refs: visibilities(*refs, panels=panels, scale=spe...]
    mul x1 -> x0, local copies, waits for them, and re-layouts: 19.9 us -> none  [body(): return picked * spectra_all ** (-0.5)]
    mul x1 -> x0, other arithmetic: 17.3 us -> none  [body(): return picked * spectra_all ** (-0.5)]
    all_to_all x4 -> x1, starting transfers between devices: 25.3 us -> 12 us  [body(): lax.all_to_all(voltages.transpose(1, 0, 2, 3), AXES, split_axis=0, concat...]
  transfers between devices with their start and end apart: 4 -> 1, of which waited for: 4 -> 1; matrix products, arithmetic and copies ran while one was open for 0% -> 0% of each run, Pallas kernels for 0% -> 0%
where the time goes in v1:
time: 91.6 us; the launch traced here: 91.4 us
  waiting for transfers between devices  52.4 us (57%)
  Pallas kernels  21.8 us (24%)
  starting transfers between devices  12 us (13%)
  local copies, waits for them, and re-layouts  4.85 us (5%)
    all_to_all x1, waiting for transfers between devices, body(): lax.all_to_all(voltages.transpose(1, 0, 2, 3), AXES, split_axis=0, concat...  52.4 us
    pallas_call x1, Pallas kernels, body(): pl.pallas_call(lambda *refs: visibilities(*refs, panels=panels, scale=spe...  21.8 us
    all_to_all x1, starting transfers between devices, body(): lax.all_to_all(voltages.transpose(1, 0, 2, 3), AXES, split_axis=0, concat...  12 us
    unnamed x3, local copies, waits for them, and re-layouts  4.85 us
  transfers between devices with their start and end apart: 1, of which 1 were waited for; matrix products, arithmetic and copies ran while one was open for 0% of the time, Pallas kernels for 0%

profile of v1, /device:TPU:1, one launch (start us, length us, event | category | flops | bytes accessed | tf_op | source)
XLA Modules:
  0.0 91.4 jit_solution(3079479327459768156)
XLA Ops:
  0.0 4.8 %copy.6 = bf16[2,128,16,512]{3,2,0,1:T(8,128)(2,1)} copy(bf16[2,128,16,512]{3,2,1,0:T(8,128)(2,1)} %param.2) | data formatting | bytes 8388608 | tf_op args[0]
  4.8 0.0 copy-start
  4.8 12.0 %all-to-all-start = ((bf16[128,2,16,512]{3,2,1,0:T(8,128)(2,1)}), bf16[128,2,16,512]{3,2,1,0:T(8,128)(2,1)}, u32[]{:S(2)}, u32[]{:S(2)}) async-start(bf16[128,2,16,512]{3,2,1,0:T(8,128)(2,1)} %bitcast.3), calls=%async_computation | async-start | bytes 8388608 | tf_op jit(solution)/shard_map/all_to_all | solution.py:79
  16.8 0.0 copy-done
  16.8 0.3 select_reduce_fusion.refs_0_
  17.1 52.4 %all-to-all-done.refs_1_ = bf16[128,2,16,512]{3,2,1,0:T(8,128)(2,1)} async-done(((bf16[128,2,16,512]{3,2,1,0:T(8,128)(2,1)}), bf16[128,2,16,512]{3,2,1,0:T(8,128)(2,1)}, u32[]{:S(2)}, u32[]{:S(2)}) %all-to-all-start) | async-done | bytes 4194336 | tf_op jit(solution)/shard_map/all_to_all | solution.py:79
  69.6 21.8 %visibilities.1 = f32[528,1,64,128]{3,2,1,0:T(8,128)} custom-call(s32[1024]{0:T(1024)S(1)} %select_reduce_fusion.refs_0_, bf16[128,2,16,512]{3,2,1,0:T(8,128)(2,1)} %all-to-all-done.refs_1_), custom_call_target="tpu_custom_call" | custom-call | flops 8858370048 | bytes 17301504 | tf_op jit(solution)/shard_map/visibilities/pallas_call | solution.py:82
  (1 shorter events, 0.0 us)
Async XLA Ops:
  4.8 12.0 %copy-start = (s32[528,2]{0,1:T(2,128)S(1)}, s32[528,2]{0,1:T(2,128)}, u32[]{:S(2)}) copy-start(s32[528,2]{0,1:T(2,128)} %param.3) | copy-start | bytes 12676
  4.8 64.7 %all-to-all-start = ((bf16[128,2,16,512]{3,2,1,0:T(8,128)(2,1)}), bf16[128,2,16,512]{3,2,1,0:T(8,128)(2,1)}, u32[]{:S(2)}, u32[]{:S(2)}) async-start(bf16[128,2,16,512]{3,2,1,0:T(8,128)(2,1)} %bitcast.3), calls=%async_computation | async-start | bytes 8388608 | tf_op jit(solution)/shard_map/all_to_all | solution.py:79

commit v2 on v1

v2 whole, which is shorter than its diff:
```python
import jax
import jax.numpy as jnp
from jax import lax
from jax.experimental import pallas as pl
from jax.experimental.pallas import tpu as pltpu
from jax.sharding import PartitionSpec as P

AXES = ("chan", "tile")
PANEL = 64
LANES = 128
GROUP = 4
DEEP = 256
UNITS = 2


def by_channel(x_ref, y_ref, sem):
    parts, _, _, spectra = x_ref.shape
    for c in range(parts):
        for k in range(spectra // LANES):
            pltpu.make_async_copy(
                x_ref.at[c, :, :, pl.ds(k * LANES, LANES)], y_ref.at[:, c, k], sem
            ).start()
    pltpu.make_async_copy(y_ref, y_ref, sem).wait()


def visibilities(slot_ref, x_ref, out_ref, staged, sem, *, panels, scale):
    per_panel = PANEL // x_ref.shape[3]
    deep_per_part = x_ref.shape[2] * LANES // DEEP
    deeps = 2 * deep_per_part
    wide = DEEP // (2 * PANEL)

    def samples(first, last, part, deep):
        halves = [
            x_ref[first * per_panel : last * per_panel, part, deep * DEEP // LANES + h]
            .reshape((last - first) * PANEL, LANES)
            for h in range(DEEP // LANES)
        ]
        return jnp.concatenate(halves, axis=1)

    def left(first, deep):
        return samples(first, first + GROUP, deep // deep_per_part, deep % deep_per_part)

    def right(first, deep):
        part, deep = deep // deep_per_part, deep % deep_per_part
        rows = []
        for q in range(first, first + wide):
            if part == 0:
                rows += [samples(q, q + 1, 0, deep), -samples(q, q + 1, 1, deep)]
            else:
                rows += [samples(q, q + 1, 1, deep), samples(q, q + 1, 0, deep)]
        return jnp.concatenate(rows, axis=0)

    steps = [
        (i, j) for j in range(panels // GROUP) for i in range(j + 1)
    ]

    def run(*sums):
        def start(tiles):
            for place, p, q in tiles:
                pltpu.make_async_copy(
                    staged.at[place], out_ref.at[slot_ref[p * panels + q], 0], sem
                ).start()

        def drain(step):
            i, j = steps[step]
            tiles = []
            for unit in range(UNITS):
                product = pltpu.matmul_pop(sums[2 * unit + step % 2]) * scale
                for a in range(GROUP):
                    for b in range(wide):
                        p, q = i * GROUP + a, j * GROUP + unit * wide + b
                        place = (step * GROUP + a) * GROUP + unit * wide + b
                        staged[place] = product[
                            a * PANEL : (a + 1) * PANEL, b * 2 * PANEL : (b + 1) * 2 * PANEL
                        ]
                        if p <= q:
                            tiles.append((place, p, q))
            return tiles

        ready = []
        for step, (i, j) in enumerate(steps):
            start(ready)
            for deep in range(deeps):
                held = deep % 2
                for unit in range(UNITS):
                    pltpu.matmul_push_rhs(
                        right(j * GROUP + unit * wide, deep), held, unit, transpose=True
                    )
                rows = left(i * GROUP, deep)
                for unit in range(UNITS):
                    pltpu.matmul_acc_lhs(sums[2 * unit + step % 2], rows, load_staged_rhs=held)
            ready = drain(step - 1) if step else []
        start(ready)
        start(drain(len(steps) - 1))

    pl.run_scoped(
        run,
        *[
            pltpu.ACC(unit)((GROUP * PANEL, DEEP), jnp.float32)
            for unit in range(UNITS)
            for _ in range(2)
        ],
    )
    pltpu.make_async_copy(out_ref, out_ref, sem).wait()


def body(voltages, tile_pairs):
    parts, chans, inputs_here, spectra = voltages.shape
    devices = lax.axis_size("chan") * lax.axis_size("tile")
    slots = tile_pairs.shape[0]
    panels = devices * inputs_here // PANEL
    blocks = panels // GROUP

    place = tile_pairs[:, 0] * panels + tile_pairs[:, 1]
    found = place[None, :] == jnp.arange(panels * panels, dtype=jnp.int32)[:, None]
    slot_of = jnp.sum(
        jnp.where(found, jnp.arange(slots, dtype=jnp.int32)[None, :], 0), axis=1
    )

    sent = pl.pallas_call(
        by_channel,
        out_shape=pltpu.VMEM(
            (chans, parts, spectra // LANES, inputs_here, LANES), voltages.dtype
        ),
        in_specs=[pl.BlockSpec(memory_space=pltpu.HBM)],
        out_specs=pl.BlockSpec(memory_space=pltpu.VMEM),
        scratch_shapes=[pltpu.SemaphoreType.DMA],
        compiler_params=pltpu.CompilerParams(vmem_limit_bytes=2**20),
        name="by_channel",
    )(pltpu.with_memory_space_constraint(voltages, pltpu.HBM))
    sent, slot_of = lax.optimization_barrier((sent, slot_of))
    turned = lax.all_to_all(sent, AXES, split_axis=0, concat_axis=0, tiled=True)
    turned = pltpu.with_memory_space_constraint(turned, pltpu.VMEM)
    return pl.pallas_call(
        lambda *refs: visibilities(*refs, panels=panels, scale=spectra**-0.5),
        out_shape=jax.ShapeDtypeStruct((slots, 1, PANEL, 2 * PANEL), jnp.float32),
        in_specs=[
            pl.BlockSpec(memory_space=pltpu.SMEM),
            pl.BlockSpec(memory_space=pltpu.VMEM),
        ],
        out_specs=pl.BlockSpec(memory_space=pl.ANY),
        scratch_shapes=[
            pltpu.VMEM((blocks * (blocks + 1) // 2 * GROUP * GROUP, PANEL, 2 * PANEL), jnp.float32),
            pltpu.SemaphoreType.DMA,
        ],
        compiler_params=pltpu.CompilerParams(vmem_limit_bytes=24 * 2**20),
        cost_estimate=pl.CostEstimate(
            flops=2 * slots * PANEL * 2 * PANEL * 2 * spectra,
            bytes_accessed=slots * PANEL * 2 * PANEL * 4,
            transcendentals=0,
        ),
        name="visibilities",
    )(slot_of, turned)


def solution(mesh):
    placed = (P(None, None, AXES, None), P())
    return jax.shard_map(
        body,
        mesh=mesh,
        in_specs=placed,
        out_specs=P(None, AXES, None, None),
        check_vma=False,
    )
```

time: 91.6 us -> 79.3 us (0.87)
  blocking collectives: 0 us -> 64.4 us
  waiting for transfers between devices: 52.4 us -> 0 us
  starting transfers between devices: 12 us -> 0 us
  Pallas kernels: 21.8 us -> 13.7 us
  local copies, waits for them, and re-layouts: 4.85 us -> 0 us
    all_to_all x0 -> x1, blocking collectives: none -> 64.4 us  [body(): turned = lax.all_to_all(sent, AXES, split_axis=0, concat_axis=0, tiled=True)]
    all_to_all x1 -> x0, waiting for transfers between devices: 52.4 us -> none  [body(): lax.all_to_all(voltages.transpose(1, 0, 2, 3), AXES, split_axis=0, concat...]
    all_to_all x1 -> x0, starting transfers between devices: 12 us -> none  [body(): lax.all_to_all(voltages.transpose(1, 0, 2, 3), AXES, split_axis=0, concat...]
    pallas_call x1, Pallas kernels: 21.8 us -> 11.3 us  [body(): pl.pallas_call(lambda *refs: visibilities(*refs, panels=panels, scale=spe...]
    unnamed x3 -> x0, local copies, waits for them, and re-layouts: 4.85 us -> none
    pallas_call x0 -> x1, Pallas kernels: none -> 2.31 us  [body(): pl.pallas_call(by_channel, out_shape=pltpu.VMEM((chans, parts, spectra //...]
  transfers between devices with their start and end apart: 1 -> 0, of which waited for: 1 -> 0; matrix products, arithmetic and copies ran while one was open for 0% -> 0% of each run, Pallas kernels for 0% -> 0%
where the time goes in v2:
time: 79.3 us; the launch traced here: 79.2 us
  blocking collectives  64.4 us (81%)
  Pallas kernels  13.7 us (17%)
  other arithmetic  1.07 us (1%)
    all_to_all x1, blocking collectives, body(): turned = lax.all_to_all(sent, AXES, split_axis=0, concat_axis=0, tiled=True)  64.4 us
    pallas_call x1, Pallas kernels, body(): pl.pallas_call(lambda *refs: visibilities(*refs, panels=panels, scale=spe...  11.3 us
    pallas_call x1, Pallas kernels, body(): pl.pallas_call(by_channel, out_shape=pltpu.VMEM((chans, parts, spectra //...  2.31 us

profile of v2, /device:TPU:1, one launch (start us, length us, event | category | flops | bytes accessed | tf_op | source)
XLA Modules:
  0.0 79.2 jit_solution(10896525159396925337)
XLA Ops:
  0.0 0.8 add_reduce_fusion
  0.8 0.3 select_reduce_fusion.refs_0_
  1.1 2.3 %by_channel.1 = bf16[128,2,4,16,128]{4,3,2,1,0:T(8,128)(2,1)S(1)} custom-call(bf16[2,128,16,512]{3,2,1,0:T(8,128)(2,1)} %x_ref.1), custom_call_target="tpu_custom_call" | custom-call | tf_op jit(solution)/shard_map/by_channel/pallas_call | solution.py:120
  3.4 64.4 %all_to_all.5.refs_1_ = bf16[128,2,4,16,128]{4,3,2,1,0:T(8,128)(2,1)S(1)} all-to-all(bf16[128,2,4,16,128]{4,3,2,1,0:T(8,128)(2,1)S(1)} %by_channel.1), channel_id=1, replica_groups=mesh['chan'=4,'tile'=32] {'chan','tile'}, dimensions={0} | all-to-all | bytes 8388608 | tf_op jit(solution)/shard_map/all_to_all | solution.py:132
  67.8 11.3 %visibilities.1 = f32[528,1,64,128]{3,2,1,0:T(8,128)} custom-call(s32[1024]{0:T(1024)S(1)} %select_reduce_fusion.refs_0_, bf16[128,2,4,16,128]{4,3,2,1,0:T(8,128)(2,1)S(1)} %all_to_all.5.refs_1_), custom_call_target="tpu_custom_call" | custom-call | flops 8858370048 | bytes 17301504 | tf_op jit(solution)/shard_map/visibilities/pallas_call | solution.py:134

commit v3 on v2

v3 whole, which is shorter than its diff:
```python
import jax
import jax.numpy as jnp
from jax import lax
from jax.experimental import pallas as pl
from jax.experimental.pallas import tpu as pltpu
from jax.sharding import PartitionSpec as P

AXES = ("chan", "tile")
PANEL = 64
LANES = 128
DEEP = 256
UNITS = 2
WIDE = DEEP // (2 * PANEL)
TALL = 2
HELD = 4


def by_channel(x_ref, pairs_ref, y_ref, slot_ref, pairs, sem, pairs_sem, *, panels):
    parts, _, _, spectra = x_ref.shape
    fetch = pltpu.make_async_copy(pairs_ref, pairs, pairs_sem)
    fetch.start()
    for c in range(parts):
        for k in range(spectra // LANES):
            pltpu.make_async_copy(
                x_ref.at[c, :, :, pl.ds(k * LANES, LANES)], y_ref.at[:, c, k], sem
            ).start()
    fetch.wait()
    here = lax.broadcasted_iota(jnp.int32, slot_ref.shape, 0) * LANES
    here = here + lax.broadcasted_iota(jnp.int32, slot_ref.shape, 1)

    def note(s, slots):
        return jnp.where(here == pairs[0, s] * panels + pairs[1, s], s, slots)

    slot_ref[...] = lax.fori_loop(0, pairs.shape[1], note, jnp.zeros_like(here), unroll=16)
    pltpu.make_async_copy(y_ref, y_ref, sem).wait()


def visibilities(slot_ref, x_ref, out_ref, staged, sem, *, panels, scale):
    per_panel = PANEL // x_ref.shape[3]
    deep_per_part = x_ref.shape[2] * LANES // DEEP
    deeps = 2 * deep_per_part

    def samples(first, count, part, deep):
        halves = [
            x_ref[first * per_panel : (first + count) * per_panel, part, deep * DEEP // LANES + h]
            .reshape(count * PANEL, LANES)
            for h in range(DEEP // LANES)
        ]
        return jnp.concatenate(halves, axis=1)

    def left(piece, deep):
        return samples(piece * TALL, TALL, deep // deep_per_part, deep % deep_per_part)

    def right(column, deep):
        part, deep = deep // deep_per_part, deep % deep_per_part
        rows = []
        for q in range(column * WIDE, (column + 1) * WIDE):
            if part == 0:
                rows += [samples(q, 1, 0, deep), -samples(q, 1, 1, deep)]
            else:
                rows += [samples(q, 1, 1, deep), samples(q, 1, 0, deep)]
        return jnp.concatenate(rows, axis=0)

    tasks = [[] for _ in range(UNITS)]
    place_of = {}
    for column in range(panels // WIDE):
        unit = (column + column // UNITS) % UNITS
        pieces = range(((column + 1) * WIDE - 1) // TALL + 1)
        for first in range(0, len(pieces), HELD):
            tasks[unit].append((column, pieces[first : first + HELD]))
        for piece in pieces:
            place_of[column, piece] = len(place_of) * TALL * WIDE

    def run(*sums):
        def total(unit, turn, n):
            return sums[(unit * 2 + turn % 2) * HELD + n]

        def start(tiles):
            for place, p, q in tiles:
                at = p * panels + q
                slot = slot_ref[at // LANES, at % LANES]
                pltpu.make_async_copy(staged.at[place], out_ref.at[slot, 0], sem).start()

        def drain(turn):
            tiles = []
            for unit in range(UNITS):
                if not 0 <= turn < len(tasks[unit]):
                    continue
                column, pieces = tasks[unit][turn]
                for n, piece in enumerate(pieces):
                    product = pltpu.matmul_pop(total(unit, turn, n)) * scale
                    for a in range(TALL):
                        for b in range(WIDE):
                            place = place_of[column, piece] + a * WIDE + b
                            staged[place] = product[
                                a * PANEL : (a + 1) * PANEL, b * 2 * PANEL : (b + 1) * 2 * PANEL
                            ]
                            p, q = piece * TALL + a, column * WIDE + b
                            if p <= q:
                                tiles.append((place, p, q))
            return tiles

        ready = []
        for turn in range(max(map(len, tasks)) + 1):
            start(ready)
            now = [(u, *tasks[u][turn]) for u in range(UNITS) if turn < len(tasks[u])]
            for deep in range(deeps):
                held = deep % 2
                for unit, column, _ in now:
                    pltpu.matmul_push_rhs(right(column, deep), held, unit, transpose=True)
                for n in range(HELD):
                    for unit, _, pieces in now:
                        if n < len(pieces):
                            pltpu.matmul_acc_lhs(
                                total(unit, turn, n),
                                left(pieces[n], deep),
                                load_staged_rhs=None if n else held,
                            )
            ready = drain(turn - 1)
        start(ready)

    pl.run_scoped(
        run,
        *[
            pltpu.ACC(unit)((TALL * PANEL, DEEP), jnp.float32)
            for unit in range(UNITS)
            for _ in range(2 * HELD)
        ],
    )
    pltpu.make_async_copy(out_ref, out_ref, sem).wait()


def body(voltages, tile_pairs):
    parts, chans, inputs_here, spectra = voltages.shape
    devices = lax.axis_size("chan") * lax.axis_size("tile")
    slots = tile_pairs.shape[0]
    panels = devices * inputs_here // PANEL
    tiles = sum(
        (((column + 1) * WIDE - 1) // TALL + 1) * TALL * WIDE for column in range(panels // WIDE)
    )

    sent, slot_of = pl.pallas_call(
        lambda *refs: by_channel(*refs, panels=panels),
        out_shape=(
            pltpu.VMEM((chans, parts, spectra // LANES, inputs_here, LANES), voltages.dtype),
            jax.ShapeDtypeStruct((panels * panels // LANES, LANES), jnp.int32),
        ),
        in_specs=[
            pl.BlockSpec(memory_space=pltpu.HBM),
            pl.BlockSpec(memory_space=pltpu.HBM),
        ],
        out_specs=(
            pl.BlockSpec(memory_space=pltpu.VMEM),
            pl.BlockSpec(memory_space=pltpu.VMEM),
        ),
        scratch_shapes=[
            pltpu.SMEM((2, slots), jnp.int32),
            pltpu.SemaphoreType.DMA,
            pltpu.SemaphoreType.DMA,
        ],
        compiler_params=pltpu.CompilerParams(vmem_limit_bytes=2**20),
        name="by_channel",
    )(
        pltpu.with_memory_space_constraint(voltages, pltpu.HBM),
        pltpu.with_memory_space_constraint(tile_pairs.T, pltpu.HBM),
    )
    turned = lax.all_to_all(sent, AXES, split_axis=0, concat_axis=0, tiled=True)
    turned = pltpu.with_memory_space_constraint(turned, pltpu.VMEM)
    return pl.pallas_call(
        lambda *refs: visibilities(*refs, panels=panels, scale=spectra**-0.5),
        out_shape=jax.ShapeDtypeStruct((slots, 1, PANEL, 2 * PANEL), jnp.float32),
        in_specs=[
            pl.BlockSpec(memory_space=pltpu.SMEM),
            pl.BlockSpec(memory_space=pltpu.VMEM),
        ],
        out_specs=pl.BlockSpec(memory_space=pl.ANY),
        scratch_shapes=[
            pltpu.VMEM((tiles, PANEL, 2 * PANEL), jnp.float32),
            pltpu.SemaphoreType.DMA,
        ],
        compiler_params=pltpu.CompilerParams(vmem_limit_bytes=24 * 2**20),
        cost_estimate=pl.CostEstimate(
            flops=2 * slots * PANEL * 2 * PANEL * 2 * spectra,
            bytes_accessed=slots * PANEL * 2 * PANEL * 4,
            transcendentals=0,
        ),
        name="visibilities",
    )(slot_of, turned)


def solution(mesh):
    placed = (P(None, None, AXES, None), P())
    return jax.shard_map(
        body,
        mesh=mesh,
        in_specs=placed,
        out_specs=P(None, AXES, None, None),
        check_vma=False,
    )
```

time: 79.3 us -> 78.4 us (0.989)
  other arithmetic: 1.07 us -> 0 us
where the time goes in v3:
time: 78.4 us; the launch traced here: 78.2 us
  blocking collectives  64.4 us (82%)
  Pallas kernels  13.8 us (18%)
    all_to_all x1, blocking collectives, body(): turned = lax.all_to_all(sent, AXES, split_axis=0, concat_axis=0, tiled=True)  64.4 us
    pallas_call x1, Pallas kernels, body(): pl.pallas_call(lambda *refs: visibilities(*refs, panels=panels, scale=spe...  11.3 us
    pallas_call x1, Pallas kernels, body(): pl.pallas_call(lambda *refs: by_channel(*refs, panels=panels), out_shape=...  2.53 us

profile of v3, /device:TPU:1, one launch (start us, length us, event | category | flops | bytes accessed | tf_op | source)
XLA Modules:
  0.0 78.2 jit_solution(14203284753060642583)
XLA Ops:
  0.0 2.5 %by_channel.1 = (bf16[128,2,4,16,128]{4,3,2,1,0:T(8,128)(2,1)S(1)}, s32[8,128]{1,0:T(8,128)S(1)}) custom-call(bf16[2,128,16,512]{3,2,1,0:T(8,128)(2,1)} %refs_0_.1, s32[2,528]{1,0:T(2,128)} %bitcast.1), custom_call_target="tpu_custom_call" | custom-call | tf_op jit(solution)/shard_map/by_channel/pallas_call | solution.py:142
  2.5 64.4 %all_to_all.5.refs_1_ = bf16[128,2,4,16,128]{4,3,2,1,0:T(8,128)(2,1)S(1)} all-to-all(bf16[128,2,4,16,128]{4,3,2,1,0:T(8,128)(2,1)S(1)} %get-tuple-element.8), channel_id=1, replica_groups=mesh['chan'=4,'tile'=32] {'chan','tile'}, dimensions={0} | all-to-all | bytes 8388608 | tf_op jit(solution)/shard_map/all_to_all | solution.py:167
  67.0 11.3 %visibilities.1 = f32[528,1,64,128]{3,2,1,0:T(8,128)} custom-call(s32[8,128]{1,0:T(8,128)S(1)} %get-tuple-element.7.refs_0_, bf16[128,2,4,16,128]{4,3,2,1,0:T(8,128)(2,1)S(1)} %all_to_all.5.refs_1_), custom_call_target="tpu_custom_call" | custom-call | flops 8858370048 | bytes 17301504 | tf_op jit(solution)/shard_map/visibilities/pallas_call | solution.py:169

commit v4 on v3

--- a/solution.py
+++ b/solution.py
@@ -25,17 +25,25 @@
                 x_ref.at[c, :, :, pl.ds(k * LANES, LANES)], y_ref.at[:, c, k], sem
             ).start()
     fetch.wait()
-    here = lax.broadcasted_iota(jnp.int32, slot_ref.shape, 0) * LANES
-    here = here + lax.broadcasted_iota(jnp.int32, slot_ref.shape, 1)
-
-    def note(s, slots):
-        return jnp.where(here == pairs[0, s] * panels + pairs[1, s], s, slots)
-
-    slot_ref[...] = lax.fori_loop(0, pairs.shape[1], note, jnp.zeros_like(here), unroll=16)
+    panel = lax.broadcasted_iota(jnp.int32, (panels, pairs.shape[1]), 0)
+    slot = lax.broadcasted_iota(jnp.int32, panel.shape, 1)
+    first, second = panel == pairs[0:1], panel == pairs[1:2]
+
+    def spread(value):
+        return lax.dot_general(
+            jnp.where(first, value, 0).astype(jnp.bfloat16),
+            jnp.where(second, 1, 0).astype(jnp.bfloat16),
+            (((1,), (1,)), ((), ())),
+            preferred_element_type=jnp.float32,
+        ).astype(jnp.int32)
+
+    slot_ref[...] = jnp.minimum(
+        spread(slot // 16) * 16 + spread(slot % 16), pairs.shape[1] - 1
+    )
     pltpu.make_async_copy(y_ref, y_ref, sem).wait()
 
 
-def visibilities(slot_ref, x_ref, out_ref, staged, sem, *, panels, scale):
+def visibilities(slots_ref, x_ref, out_ref, slot_of, staged, slot_sem, sem, *, panels, scale):
     per_panel = PANEL // x_ref.shape[3]
     deep_per_part = x_ref.shape[2] * LANES // DEEP
     deeps = 2 * deep_per_part
@@ -77,9 +85,9 @@
 
         def start(tiles):
             for place, p, q in tiles:
-                at = p * panels + q
-                slot = slot_ref[at // LANES, at % LANES]
-                pltpu.make_async_copy(staged.at[place], out_ref.at[slot, 0], sem).start()
+                pltpu.make_async_copy(
+                    staged.at[place], out_ref.at[slot_of[p, q], 0], sem
+                ).start()
 
         def drain(turn):
             tiles = []
@@ -100,8 +108,12 @@
                                 tiles.append((place, p, q))
             return tiles
 
+        fetch = pltpu.make_async_copy(slots_ref, slot_of, slot_sem)
+        fetch.start()
         ready = []
         for turn in range(max(map(len, tasks)) + 1):
+            if turn == 2:
+                fetch.wait()
             start(ready)
             now = [(u, *tasks[u][turn]) for u in range(UNITS) if turn < len(tasks[u])]
             for deep in range(deeps):
@@ -139,11 +151,11 @@
         (((column + 1) * WIDE - 1) // TALL + 1) * TALL * WIDE for column in range(panels // WIDE)
     )
 
-    sent, slot_of = pl.pallas_call(
+    sent, slots_of = pl.pallas_call(
         lambda *refs: by_channel(*refs, panels=panels),
         out_shape=(
             pltpu.VMEM((chans, parts, spectra // LANES, inputs_here, LANES), voltages.dtype),
-            jax.ShapeDtypeStruct((panels * panels // LANES, LANES), jnp.int32),
+            jax.ShapeDtypeStruct((panels, panels), jnp.int32),
         ),
         in_specs=[
             pl.BlockSpec(memory_space=pltpu.HBM),
@@ -154,7 +166,7 @@
             pl.BlockSpec(memory_space=pltpu.VMEM),
         ),
         scratch_shapes=[
-            pltpu.SMEM((2, slots), jnp.int32),
+            pltpu.VMEM((2, slots), jnp.int32),
             pltpu.SemaphoreType.DMA,
             pltpu.SemaphoreType.DMA,
         ],
@@ -170,12 +182,14 @@
         lambda *refs: visibilities(*refs, panels=panels, scale=spectra**-0.5),
         out_shape=jax.ShapeDtypeStruct((slots, 1, PANEL, 2 * PANEL), jnp.float32),
         in_specs=[
-            pl.BlockSpec(memory_space=pltpu.SMEM),
+            pl.BlockSpec(memory_space=pl.ANY),
             pl.BlockSpec(memory_space=pltpu.VMEM),
         ],
         out_specs=pl.BlockSpec(memory_space=pl.ANY),
         scratch_shapes=[
+            pltpu.SMEM((panels, panels), jnp.int32),
             pltpu.VMEM((tiles, PANEL, 2 * PANEL), jnp.float32),
+            pltpu.SemaphoreType.DMA,
             pltpu.SemaphoreType.DMA,
         ],
         compiler_params=pltpu.CompilerParams(vmem_limit_bytes=24 * 2**20),
@@ -185,7 +199,7 @@
             transcendentals=0,
         ),
         name="visibilities",
-    )(slot_of, turned)
+    )(slots_of, turned)
 
 
 def solution(mesh):

time: 78.4 us -> 77.7 us (level)
  no operation moved by 1% of the time
where the time goes in v4:
time: 77.7 us; the launch traced here: 77.6 us
  blocking collectives  64.4 us (83%)
  Pallas kernels  13.1 us (17%)
    all_to_all x1, blocking collectives, body(): turned = lax.all_to_all(sent, AXES, split_axis=0, concat_axis=0, tiled=True)  64.4 us
    pallas_call x1, Pallas kernels, body(): pl.pallas_call(lambda *refs: visibilities(*refs, panels=panels, scale=spe...  10.8 us
    pallas_call x1, Pallas kernels, body(): pl.pallas_call(lambda *refs: by_channel(*refs, panels=panels), out_shape=...  2.33 us

profile of v4, /device:TPU:1, one launch (start us, length us, event | category | flops | bytes accessed | tf_op | source)
XLA Modules:
  0.0 77.6 jit_solution(2872733355476717464)
XLA Ops:
  0.0 2.3 %by_channel.1 = (bf16[128,2,4,16,128]{4,3,2,1,0:T(8,128)(2,1)S(1)}, s32[32,32]{1,0:T(8,128)S(1)}) custom-call(bf16[2,128,16,512]{3,2,1,0:T(8,128)(2,1)} %refs_0_.1, s32[2,528]{1,0:T(2,128)} %bitcast.1), custom_call_target="tpu_custom_call" | custom-call | tf_op jit(solution)/shard_map/by_channel/pallas_call | solution.py:154
  2.3 64.4 %all_to_all.5.refs_1_ = bf16[128,2,4,16,128]{4,3,2,1,0:T(8,128)(2,1)S(1)} all-to-all(bf16[128,2,4,16,128]{4,3,2,1,0:T(8,128)(2,1)S(1)} %get-tuple-element.8), channel_id=1, replica_groups=mesh['chan'=4,'tile'=32] {'chan','tile'}, dimensions={0} | all-to-all | bytes 8388608 | tf_op jit(solution)/shard_map/all_to_all | solution.py:179
  66.8 10.8 %visibilities.1 = f32[528,1,64,128]{3,2,1,0:T(8,128)} custom-call(s32[32,32]{1,0:T(8,128)S(1)} %get-tuple-element.7.refs_0_, bf16[128,2,4,16,128]{4,3,2,1,0:T(8,128)(2,1)S(1)} %all_to_all.5.refs_1_), custom_call_target="tpu_custom_call" | custom-call | flops 8858370048 | bytes 17301504 | tf_op jit(solution)/shard_map/visibilities/pallas_call | solution.py:181

commit v5 on v4

--- a/solution.py
+++ b/solution.py
@@ -1,5 +1,6 @@
 import jax
 import jax.numpy as jnp
+import numpy as np
 from jax import lax
 from jax.experimental import pallas as pl
 from jax.experimental.pallas import tpu as pltpu
@@ -10,20 +11,25 @@
 LANES = 128
 DEEP = 256
 UNITS = 2
+CORES = 2
 WIDE = DEEP // (2 * PANEL)
 TALL = 2
 HELD = 4
 
 
 def by_channel(x_ref, pairs_ref, y_ref, slot_ref, pairs, sem, pairs_sem, *, panels):
-    parts, _, _, spectra = x_ref.shape
+    parts, spectra = x_ref.shape[0], x_ref.shape[-1]
     fetch = pltpu.make_async_copy(pairs_ref, pairs, pairs_sem)
     fetch.start()
     for c in range(parts):
         for k in range(spectra // LANES):
-            pltpu.make_async_copy(
-                x_ref.at[c, :, :, pl.ds(k * LANES, LANES)], y_ref.at[:, c, k], sem
-            ).start()
+            for x in range(y_ref.shape[3]):
+                for core in range(y_ref.shape[1]):
+                    pltpu.make_async_copy(
+                        x_ref.at[c, x, :, :, core, :, pl.ds(k * LANES, LANES)],
+                        y_ref.at[:, core, :, x, c, k],
+                        sem,
+                    ).start()
     fetch.wait()
     panel = lax.broadcasted_iota(jnp.int32, (panels, pairs.shape[1]), 0)
     slot = lax.broadcasted_iota(jnp.int32, panel.shape, 1)
@@ -44,16 +50,21 @@
 
 
 def visibilities(slots_ref, x_ref, out_ref, slot_of, staged, slot_sem, sem, *, panels, scale):
-    per_panel = PANEL // x_ref.shape[3]
-    deep_per_part = x_ref.shape[2] * LANES // DEEP
+    ys, cores, zs, _, _, blocks, inputs_here, _ = x_ref.shape
+    chips_per_panel = PANEL // (cores * inputs_here)
+    deep_per_part = blocks * LANES // DEEP
     deeps = 2 * deep_per_part
 
     def samples(first, count, part, deep):
-        halves = [
-            x_ref[first * per_panel : (first + count) * per_panel, part, deep * DEEP // LANES + h]
-            .reshape(count * PANEL, LANES)
-            for h in range(DEEP // LANES)
-        ]
+        chips = range(first * chips_per_panel, (first + count) * chips_per_panel)
+        halves = []
+        for k in range(deep * DEEP // LANES, (deep + 1) * DEEP // LANES):
+            rows = [
+                x_ref[chip // zs % ys, core, chip % zs, chip // zs // ys, part, k]
+                for chip in chips
+                for core in range(cores)
+            ]
+            halves.append(jnp.concatenate(rows, axis=0))
         return jnp.concatenate(halves, axis=1)
 
     def left(piece, deep):
@@ -144,7 +155,10 @@
 
 def body(voltages, tile_pairs):
     parts, chans, inputs_here, spectra = voltages.shape
-    devices = lax.axis_size("chan") * lax.axis_size("tile")
+    xs, tiles_of_x = lax.axis_size("chan"), lax.axis_size("tile")
+    devices = xs * tiles_of_x
+    ys = zs = round((tiles_of_x // CORES) ** 0.5)
+    order = np.arange(devices).reshape(xs, ys, zs, CORES).transpose(1, 3, 2, 0).reshape(-1)
     slots = tile_pairs.shape[0]
     panels = devices * inputs_here // PANEL
     tiles = sum(
@@ -154,7 +168,9 @@
     sent, slots_of = pl.pallas_call(
         lambda *refs: by_channel(*refs, panels=panels),
         out_shape=(
-            pltpu.VMEM((chans, parts, spectra // LANES, inputs_here, LANES), voltages.dtype),
+            pltpu.VMEM(
+                (ys, CORES, zs, xs, parts, spectra // LANES, inputs_here, LANES), voltages.dtype
+            ),
             jax.ShapeDtypeStruct((panels, panels), jnp.int32),
         ),
         in_specs=[
@@ -173,10 +189,19 @@
         compiler_params=pltpu.CompilerParams(vmem_limit_bytes=2**20),
         name="by_channel",
     )(
-        pltpu.with_memory_space_constraint(voltages, pltpu.HBM),
+        pltpu.with_memory_space_constraint(
+            voltages.reshape(parts, xs, ys, zs, CORES, inputs_here, spectra), pltpu.HBM
+        ),
         pltpu.with_memory_space_constraint(tile_pairs.T, pltpu.HBM),
     )
-    turned = lax.all_to_all(sent, AXES, split_axis=0, concat_axis=0, tiled=True)
+    turned = lax.all_to_all(
+        sent.reshape(chans, *sent.shape[4:]),
+        AXES,
+        split_axis=0,
+        concat_axis=0,
+        axis_index_groups=[order.tolist()],
+        tiled=True,
+    ).reshape(sent.shape)
     turned = pltpu.with_memory_space_constraint(turned, pltpu.VMEM)
     return pl.pallas_call(
         lambda *refs: visibilities(*refs, panels=panels, scale=spectra**-0.5),

time: 77.7 us -> 76.2 us (0.981)
  blocking collectives: 64.4 us -> 62.8 us
    all_to_all x1, blocking collectives: 64.4 us -> 62.8 us  [body(): lax.all_to_all(sent.reshape(chans, *sent.shape[4:]), AXES, split_axis=0,...]
where the time goes in v5:
time: 76.2 us; the launch traced here: 76 us
  blocking collectives  62.8 us (82%)
  Pallas kernels  13.2 us (17%)
    all_to_all x1, blocking collectives, body(): lax.all_to_all(sent.reshape(chans, *sent.shape[4:]), AXES, split_axis=0,...  62.8 us
    pallas_call x1, Pallas kernels, body(): pl.pallas_call(lambda *refs: visibilities(*refs, panels=panels, scale=spe...  10.8 us
    pallas_call x1, Pallas kernels, body(): pl.pallas_call(lambda *refs: by_channel(*refs, panels=panels), out_shape=...  2.4 us

profile of v5, /device:TPU:1, one launch (start us, length us, event | category | flops | bytes accessed | tf_op | source)
XLA Modules:
  0.0 76.0 jit_solution(2405101993062993263)
XLA Ops:
  0.0 2.4 %by_channel.1 = (bf16[4,2,4,4,2,4,16,128]{7,6,5,4,3,2,1,0:T(8,128)(2,1)S(1)}, s32[32,32]{1,0:T(8,128)S(1)}) custom-call(bf16[2,4,4,4,2,16,512]{6,5,4,3,2,1,0:T(8,128)(2,1)} %bitcast.6, s32[2,528]{1,0:T(2,128)} %bitcast.7), custom_call_target="tpu_custom_call" | custom-call | tf_op jit(solution)/shard_map/by_channel/pallas_call | solution.py:168
  2.4 62.8 %all_to_all.5 = bf16[128,2,4,16,128]{4,3,2,1,0:T(8,128)(2,1)S(1)} all-to-all(bf16[128,2,4,16,128]{4,3,2,1,0:T(8,128)(2,1)S(1)} %bitcast.5), channel_id=1, replica_groups={{0,32,64,96,2,34,66,98,4,36,68,100,6,38,70,102,1,33,65,97,3,35,67,99,5,..., dimensions={0} | all-to-all | bytes 8388608 | tf_op jit(solution)/shard_map/all_to_all | solution.py:197
  65.2 10.8 %visibilities.1 = f32[528,1,64,128]{3,2,1,0:T(8,128)} custom-call(s32[32,32]{1,0:T(8,128)S(1)} %get-tuple-element.7.refs_0_, bf16[4,2,4,4,2,4,16,128]{7,6,5,4,3,2,1,0:T(8,128)(2,1)S(1)} %bitcast.4), custom_call_target="tpu_custom_call" | custom-call | flops 8858370048 | bytes 17301504 | tf_op jit(solution)/shard_map/visibilities/pallas_call | solution.py:206
